TPU v7x, 512 devices: a whole 4x8x8 slice. The times are simulated.
512 devices in a mesh: inner: 64 (over y, z), res: 8 (over x, core).
Axes of the slice: x: 4, y: 8, z: 8, core: 2. Of those that a mesh axis runs over, the one named last changes fastest.
Arguments:
- left_u: bfloat16 [8, 256, 1024, 64], P('res', 'inner'), may hold values from -6 to 6
- left_v: bfloat16 [8, 256, 1024, 64], P('res', 'inner'), may hold values from -0.1875 to 0.1875
- left_rank: int32 [8, 256], P('res', 'inner'), may hold values from 1 to 64
- right_u: bfloat16 [256, 8, 1024, 64], P('inner', 'res'), may hold values from -6 to 6
- right_v: bfloat16 [256, 8, 1024, 64], P('inner', 'res'), may hold values from -0.1875 to 0.1875
- right_rank: int32 [256, 8], P('inner', 'res'), may hold values from 1 to 64
- near_tiles: bfloat16 [64, 8, 1024, 1024], P('inner', 'res'), may hold values from -4 to 4
- near_block: int32 [64, 8], P('inner', 'res'), may hold values from -1 to 3
- comp_rank: int32 [8, 8], P(None, 'res'), may hold values from 16 to 64
- omega: bfloat16 [8, 1024, 64], P('res'), may hold values from -0.1875 to 0.1875
Outputs:
- basis: float32 [8, 8, 1024, 64], P(None, 'res', 'inner')
- image: float32 [8, 8, 1024, 64], P(None, 'res', 'inner')
All inputs are finite; a program needn't handle non-finite values.
Results may differ from a plain program's by a relative error of at most 0.0059.
Values may be sent and summed in bfloat16 or wider, within the bound.
A program may use at most 64 MiB of HBM per device.

v0:
```python
import jax
import jax.numpy as jnp
from jax import lax
from jax.sharding import PartitionSpec as P


def masked(factor, rank):
    columns = jnp.arange(factor.shape[-1])
    return factor * (columns < rank[..., None, None]).astype(factor.dtype)


def gram_of(sketch):
    return jnp.einsum("ijbs,ijbt->ijst", sketch, sketch, precision=lax.Precision.HIGHEST)


def orthonormal(sketch, lower_factor):
    solved = jax.scipy.linalg.solve_triangular(lower_factor, jnp.swapaxes(sketch, 2, 3), lower=True)
    return jnp.swapaxes(solved, 2, 3)


def compress(partial_value, unused, own_rows):
    sketch = lax.psum(partial_value, "inner")
    lower_factor = jnp.linalg.cholesky(gram_of(sketch) + unused)
    basis = orthonormal(sketch, lower_factor)
    own_basis = lax.dynamic_slice_in_dim(basis, lax.axis_index("inner") * own_rows, own_rows, 2)
    return (basis, own_basis)


def local(
    left_u,
    left_v,
    left_rank,
    right_u,
    right_v,
    right_rank,
    near_tiles,
    near_block,
    comp_rank,
    omega,
):
    gathered_u, gathered_v, gathered_rank = (
        lax.all_gather(left_u, "res", axis=0, tiled=True),
        lax.all_gather(left_v, "res", axis=0, tiled=True),
        lax.all_gather(left_rank, "res", axis=0, tiled=True),
    )
    left_cut_v = masked(gathered_v, gathered_rank)
    right_cut_u = masked(right_u, right_rank)
    right_cut_v = masked(right_v, right_rank)
    blocks_here = left_u.shape[1]
    tile_size = left_u.shape[2]
    ranks_out = omega.shape[2]
    held = jnp.einsum(
        "kjbs,ikbr->ikjsr", right_cut_u, left_cut_v, preferred_element_type=jnp.float32
    ).astype(jnp.bfloat16)
    far_part = jnp.einsum(
        "kjcs,ikjsr->ikjcr", right_cut_v, held, preferred_element_type=jnp.float32
    ).astype(jnp.bfloat16)
    chosen = jnp.arange(blocks_here)[:, None] == near_block[0][None, :]
    near_rows = jnp.einsum(
        "kj,ikbr->ijbr", chosen.astype(jnp.bfloat16), left_cut_v, preferred_element_type=jnp.float32
    ).astype(jnp.bfloat16)
    near_part = jnp.einsum(
        "jbc,ijbr->ijcr", near_tiles[0], near_rows, preferred_element_type=jnp.float32
    ).astype(jnp.bfloat16)
    weight = jnp.where(chosen[None, :, :, None, None], near_part[:, None], far_part)
    active = jnp.arange(ranks_out)[None, None, :] < comp_rank[:, :, None]
    sketch_test = omega[None] * active[:, :, None, :].astype(jnp.bfloat16)
    expand = jnp.einsum(
        "ikjcr,ijcs->ikjrs", weight, sketch_test, preferred_element_type=jnp.float32
    ).astype(jnp.bfloat16)
    eye_rank = jnp.eye(ranks_out, dtype=jnp.float32)
    own_rows = tile_size // lax.axis_size("inner")
    left_cut_u = masked(gathered_u, gathered_rank)
    partial_value = jnp.einsum(
        "ikbr,ikjrs->ijbs", left_cut_u, expand, preferred_element_type=jnp.float32
    )
    unused = (1.0 - active.astype(jnp.float32))[..., None] * eye_rank
    basis, own_basis = compress(partial_value, unused, own_rows)
    basis_half = basis.astype(jnp.bfloat16)
    projected = jnp.einsum(
        "ikbr,ijbs->ikjrs", left_cut_u, basis_half, preferred_element_type=jnp.float32
    ).astype(jnp.bfloat16)
    images = lax.psum_scatter(
        jnp.einsum("ikjcr,ikjrs->cijs", weight, projected, preferred_element_type=jnp.float32),
        "inner",
        scatter_dimension=0,
        tiled=True,
    )
    return (own_basis, jnp.transpose(images, (1, 2, 0, 3)))


def solution(mesh):
    placed = (
        P("res", "inner", None, None),
        P("res", "inner", None, None),
        P("res", "inner"),
        P("inner", "res", None, None),
        P("inner", "res", None, None),
        P("inner", "res"),
        P("inner", "res", None, None),
        P("inner", "res"),
        P(None, "res"),
        P("res", None, None),
    )
    return jax.shard_map(
        local,
        mesh=mesh,
        in_specs=placed,
        out_specs=(P(None, "res", "inner", None), P(None, "res", "inner", None)),
        check_vma=False,
    )
```

profile of v0, /device:TPU:1, one launch (start us, length us, event | category | flops | bytes accessed | tf_op | source)
XLA Modules:
  0.0 619.2 jit_solution(9441940910995488083)
XLA Ops:
  7.2 0.7 all-gather.4.cloned.1.call-update
  7.9 0.0 all-gather.6.cloned.1.call-start
  8.0 0.7 all-gather.6.cloned.1.call-update
  8.7 0.0 all-reduce.2.cloned.1.call-start
  9.4 14.7 %all-gather = s32[8,1,4]{2,1,0:T(1,128)S(1)} all-gather(s32[1,1,4]{2,1,0:T(1,128)} %bitcast.137), channel_id=1, replica_groups=mesh['inner'=64,'res'=8] {'res'}, dimensions={0}, use_global_device_ids=true | all-gather | bytes 144 | tf_op jit(solution)/shard_map/all_gather | solution.py:44
  24.0 0.7 fusion.85
  24.8 0.7 fusion.84
  25.5 0.1 fusion.82
  25.6 28.0 %all-gather.4.cloned.1.call-done = bf16[8,4,1024,64]{2,3,1,0:T(8,128)(2,1)} async-done(((bf16[1,4,1024,64]{2,3,1,0:T(8,128)(2,1)}), bf16[8,4,1024,64]{2,3,1,0:T(8,128)(2,1)}) %all-gather.4.cloned.1.call-update) | async-done | bytes 4194320 | tf_op jit(solution)/shard_map/all_gather | solution.py:43
  53.5 2.5 broadcast_multiply_fusion
  56.1 3.0 fusion.3
  59.1 2.3 fusion.30
  61.4 6.9 %fusion = bf16[8,4,1024,64]{2,3,0,1:T(8,128)(2,1)} fusion(pred[4]{0:T(512)(128)(4,1)S(1)} %iota_compare_fusion.5, bf16[8,1024,64]{1,2,0:T(8,128)(2,1)} %fusion.30, bf16[8,4,1024,64]{2,3,1,0:T(8,128)(2,1)} %copy-done.1, bf16[4,1,1024,64]{2,3,1,0:T(8,128)(2,1)S(1)} %copy-done.3, bf16[4,1,1024,64]{2,3,1,0:T(8,128)(2,1)S(1)} %copy-done.4, ...), kind=kOutput, calls=%fused_computation.1 | convolution fusion | flops 541720576 | bytes 10486276 | tf_op jit(solution)/shard_map/kjcs,ikjsr->ikjcr/dot_general | solution.py:55
  68.3 24.8 %all-gather.6.cloned.1.call-done = bf16[8,4,1024,64]{2,3,1,0:T(8,128)(2,1)} async-done(((bf16[1,4,1024,64]{2,3,1,0:T(8,128)(2,1)}), bf16[8,4,1024,64]{2,3,1,0:T(8,128)(2,1)}) %all-gather.6.cloned.1.call-update) | async-done | bytes 4194320 | tf_op jit(solution)/shard_map/all_gather | solution.py:42
  93.2 7.7 %fusion.21 = f32[8,1,1024,64]{2,3,0,1:T(8,128)} fusion(bf16[8,4,1024,64]{2,3,1,0:T(8,128)(2,1)} %all-gather.6.cloned.1.call-done, bf16[8,4,64]{2,1,0:T(4,128)(2,1)S(1)} %fusion.82, bf16[8,4,1024,64]{2,3,0,1:T(8,128)(2,1)} %fusion, bf16[8,64]{1,0:T(8,128)(2,1)S(1)} %fusion.84, bf16[1024,64]{0,1:T(8,128)(2,1)S(1)} %bitcast.138), kind=kOutput, calls=%fused_computation.24 | convolution fusion | flops 541196288 | bytes 10621952 | tf_op jit(solution)/shard_map/ikbr,ikjrs->ijbs/dot_general | solution.py:74
  100.9 0.2 reduce-scatter.2.cloned.1.call-start
  101.2 0.1 copy.49
  101.3 0.1 convert_subtract_fusion
  101.4 159.0 %all-reduce.2.cloned.1.call-done = f32[8,1,1024,64]{2,3,0,1:T(8,128)} async-done(((f32[8,1,1024,64]{2,3,0,1:T(8,128)}), f32[8,1,1024,64]{2,3,0,1:T(8,128)}) %all-reduce.2.cloned.1.call-update) | async-done | bytes 2097168 | tf_op jit(solution)/shard_map/psum | solution.py:22
  260.3 4.3 fusion.51
  264.7 0.1 copy.51
  264.9 46.9 %custom-call.8 = f32[8,1,64,64]{3,2,1,0:T(8,128)S(1)} custom-call(f32[8,1,64,64]{3,2,1,0:T(8,128)S(1)} %fusion.78), custom_call_target="Cholesky" | custom-call | tf_op jit(solution)/shard_map/jit(cholesky)/cholesky | solution.py:23
  311.8 0.1 compare_reduce_fusion
  311.9 0.1 select_select_fusion
  312.0 39.3 %custom-call.9 = f32[8,1,64,64]{2,3,1,0:T(8,128)S(1)} custom-call(f32[8,1,64,64]{3,2,1,0:T(8,128)S(1)} %select_select_fusion), custom_call_target="InvertDiagBlocksLowerTriangular" | custom-call | tf_op jit(solution)/shard_map/jit(_solve_triangular)/vmap()/triangular_solve | solution.py:17
  351.4 4.9 fusion.13
  356.2 8.3 %fusion.24 = f32[1024,8,1,64]{0,3,1,2:T(8,128)} fusion(bf16[8,4,1024,64]{2,3,0,1:T(8,128)(2,1)} %fusion, bf16[8,4,1024,64]{2,3,1,0:T(8,128)(2,1)} %all-gather.6.cloned.1.call-done, bf16[8,4,64]{2,1,0:T(4,128)(2,1)S(1)} %fusion.82, f32[8,64,1024]{2,1,0:T(8,128)} %fusion.13), kind=kOutput, calls=%fused_computation.25 | convolution fusion | flops 545914880 | bytes 12587008 | tf_op jit(solution)/shard_map/ikjcr,ikjrs->cijs/dot_general | solution.py:84
  364.6 3.8 copy.55
  368.4 1.1 constant_dynamic-slice_fusion
  369.5 0.8 copy.53
  370.3 240.9 %reduce-scatter.2.cloned.1.call-done = f32[16,8,1,64]{3,1,2,0:T(8,128)} async-done(((f32[1024,8,1,64]{3,1,2,0:T(8,128)}), f32[16,8,1,64]{3,1,2,0:T(8,128)}) %reduce-scatter.2.cloned.1.call-update) | async-done | bytes 32784 | tf_op jit(solution)/shard_map/reduce_scatter | solution.py:83
  611.2 1.5 copy.56
  (21 shorter events, 0.2 us)
Async XLA Ops:
  7.2 51.9 %copy-start = (bf16[1,1,1024,1024]{3,2,1,0:T(8,128)(2,1)S(1)}, bf16[1,1,1024,1024]{3,2,1,0:T(8,128)(2,1)}, u32[]{:S(2)}) copy-start(bf16[1,1,1024,1024]{3,2,1,0:T(8,128)(2,1)} %param.16) | copy-start | bytes 6291460
  7.2 46.4 %all-gather.4.cloned.1.call-start = ((), (), s32[]{:S(2)}) async-start(), calls=%async_computation.1 | async-start | bytes 4718592 | tf_op jit(solution)/shard_map/all_gather | solution.py:43
  7.9 85.3 %all-gather.6.cloned.1.call-start = ((), (), s32[]{:S(2)}) async-start(), calls=%async_computation.2 | async-start | bytes 4718592 | tf_op jit(solution)/shard_map/all_gather | solution.py:42
  8.7 251.7 %all-reduce.2.cloned.1.call-start = ((), (), s32[]{:S(2)}) async-start(), calls=%async_computation.3 | async-start | bytes 4194304 | tf_op jit(solution)/shard_map/psum | solution.py:22
  56.1 3.0 copy-start.1
  59.1 2.3 copy-start.3
  59.1 2.3 copy-start.4
  61.4 31.8 %copy-start.5 = (bf16[1,1024,64]{1,2,0:T(8,128)(2,1)S(1)}, bf16[1,1024,64]{1,2,0:T(8,128)(2,1)}, u32[]{:S(2)}) copy-start(bf16[1,1024,64]{1,2,0:T(8,128)(2,1)} %param.19) | copy-start | bytes 393220
  93.2 8.1 %copy-start.2 = (s32[8,1]{0,1:T(1,128)S(1)}, s32[8,1]{0,1:T(1,128)}, u32[]{:S(2)}) copy-start(s32[8,1]{0,1:T(1,128)} %param.18) | copy-start | bytes 100
  100.9 510.2 %reduce-scatter.2.cloned.1.call-start = ((), (), s32[]{:S(2)}) async-start(), calls=%async_computation.4 | async-start | bytes 4259840 | tf_op jit(solution)/shard_map/reduce_scatter | solution.py:83
Sparse Core Ops, SparseCore 0:
  10.2 43.3 all-gather.3
  55.7 37.4 all-gather.5
  101.1 159.2 all-reduce.1
  368.5 242.5 reduce-scatter.1
where the time goes:
time: 623 us; the launch traced here: 619 us
  waiting for transfers between devices  454 us (73%)
  other arithmetic  90.7 us (15%)
  matrix products  37.5 us (6%)
  blocking collectives  14.7 us (2%)
  between operations  14.6 us (2%)
  local copies, waits for them, and re-layouts  7.37 us (1%)
    reduce_scatter x1, waiting for transfers between devices, local(): lax.psum_scatter(jnp.einsum('ikjcr,ikjrs->cijs', weight, projected, prefe...  241 us
    psum x1, waiting for transfers between devices, compress(): sketch = lax.psum(partial_value, 'inner')  159 us
    another operation x4, other arithmetic, compress(): lower_factor = jnp.linalg.cholesky(gram_of(sketch) + unused)  47.1 us
    another operation x3, other arithmetic, orthonormal(): jax.scipy.linalg.solve_triangular(lower_factor, jnp.swapaxes(sketch, 2, 3...  39.4 us
    all_gather x1, waiting for transfers between devices, local(): lax.all_gather(left_v, 'res', axis=0, tiled=True)  28 us
    all_gather x1, waiting for transfers between devices, local(): lax.all_gather(left_u, 'res', axis=0, tiled=True)  24.8 us
    all_gather x1, blocking collectives, local(): lax.all_gather(left_rank, 'res', axis=0, tiled=True)  14.7 us
  transfers between devices with their start and end apart: 4, of which 4 were waited for; matrix products, arithmetic and copies ran while one was open for 3% of the time, Pallas kernels for 0%

commit v1 on v0

v1 whole, which is shorter than its diff:
```python
import jax
import jax.numpy as jnp
from jax import lax
from jax.experimental import pallas as pl
from jax.experimental.pallas import tpu as pltpu
from jax.sharding import PartitionSpec as P

BF = jnp.bfloat16
F32 = jnp.float32
MESH = pl.DeviceIdType.MESH
HIGHEST = lax.Precision.HIGHEST
NY = 8
NZ = 8
NX = 4
COPIES = 160


def dot_nn(a, b, precision=None):
    return lax.dot_general(a, b, (((1,), (0,)), ((), ())), precision=precision, preferred_element_type=F32)


def dot_nt(a, b, precision=None):
    return lax.dot_general(a, b, (((1,), (1,)), ((), ())), precision=precision, preferred_element_type=F32)


def lanes(shape):
    return lax.broadcasted_iota(jnp.int32, shape, len(shape) - 1)


def row_mask(rank, shape):
    rows = lax.broadcasted_iota(jnp.int32, shape, 0)
    return jnp.where(rows < rank, 1.0, 0.0).astype(BF)


def inverse_factor(gram):
    lane32 = lanes((32, 128))
    rows32 = lax.broadcasted_iota(jnp.int32, (32, 128), 0)
    top = jnp.where(lane32 < 64, gram, jnp.where(lane32 - 64 == rows32, 1.0, 0.0))
    bottom = jnp.where(lane32 < 64, pltpu.roll(gram, 64, 1), jnp.where(lane32 - 96 == rows32, 1.0, 0.0))
    blocks = [top[8 * b : 8 * b + 8] for b in range(4)] + [bottom[8 * b : 8 * b + 8] for b in range(4)]
    rows8 = lax.broadcasted_iota(jnp.int32, (8, 128), 0)
    for k in range(64):
        kb, kr = k // 8, k % 8
        row = blocks[kb][kr : kr + 1, :]
        scaled = row / row[:, k : k + 1]
        for b in range(kb, 8):
            factor = blocks[b][:, k : k + 1]
            update = factor * scaled
            if b == kb:
                update = jnp.where(rows8 > kr, update, 0.0)
            blocks[b] = blocks[b] - update
    lane8 = lanes((8, 128))
    for b in range(8):
        diagonal = jnp.sum(jnp.where(lane8 == rows8 + 8 * b, blocks[b], 0.0), axis=1, keepdims=True)
        blocks[b] = blocks[b] * (1.0 / jnp.sqrt(diagonal))
    top = jnp.concatenate(blocks[:4], axis=0)
    bottom = jnp.concatenate(blocks[4:], axis=0)
    return jnp.where(lane32 < 64, pltpu.roll(top, 64, 1), bottom)


def block_pair(first, second):
    lane32 = lanes((32, 128))
    left = lane32 < 64
    return jnp.concatenate(
        [
            jnp.where(left, first, 0.0),
            jnp.where(left, pltpu.roll(first, 64, 1), 0.0),
            jnp.where(left, 0.0, pltpu.roll(second, 64, 1)),
            jnp.where(left, 0.0, second),
        ],
        axis=0,
    )


def kernel(
    lv_ref,
    lu_ref,
    ru_ref,
    rv_ref,
    near_ref,
    omega_ref,
    left_rank,
    right_rank,
    near_block,
    comp_rank,
    basis_ref,
    image_ref,
    lvb,
    wt,
    lum,
    rum,
    rvm,
    exs,
    exr,
    ska,
    skb,
    ra,
    rb,
    sa,
    sb,
    ra2,
    rb2,
    sfull,
    gs,
    gr,
    linvg,
    linvr,
    srr,
    ut,
    utr,
    lvsel,
    held,
    wgt,
    act,
    actr,
    ia,
    ib,
    imt,
    ria,
    rib,
    fa,
    fb,
    ria2,
    rib2,
    rows,
    send_sem,
    recv_sem,
):
    p = lax.axis_index("inner")
    r = lax.axis_index("res")
    y, z = p // NZ, p % NZ
    x, c = r // 2, r % 2
    used = [0]

    def at_y(d):
        return (lax.rem(y + d, NY) * NZ + z, r)

    def at_z(d):
        return (y * NZ + lax.rem(z + d, NZ), r)

    def at_res(q, par):
        return (p, lax.rem(x + q, NX) * 2 + (c if par == 0 else 1 - c))

    def res_of(q, par):
        return lax.rem(x + q, NX) * 2 + (c if par == 0 else 1 - c)

    def start(src, dst, device):
        n = used[0]
        used[0] += 1
        copy = pltpu.make_async_remote_copy(
            src_ref=src,
            dst_ref=dst,
            send_sem=send_sem.at[n],
            recv_sem=recv_sem.at[n],
            device_id=device,
            device_id_type=MESH,
        )
        copy.start()
        pending.append(copy)
        return copy

    pending = []
    pairs = [(q, par) for q in range(NX) for par in range(2)]
    others = pairs[1:]
    back = {(q, par): ((NX - q) % NX) * 2 + par for q, par in pairs}

    barrier = pltpu.get_barrier_semaphore()
    for d in range(1, NY):
        pl.semaphore_signal(barrier, inc=1, device_id=at_y(d), device_id_type=MESH)
    for d in range(1, NZ):
        pl.semaphore_signal(barrier, inc=1, device_id=at_z(d), device_id_type=MESH)
    for q, par in others:
        pl.semaphore_signal(barrier, inc=1, device_id=at_res(q, par), device_id_type=MESH)

    for k in range(4):
        lvb[k, 0, 0:64, :] = lv_ref[k] * row_mask(left_rank[0, k], (64, 1024))
    pl.semaphore_wait(barrier, NY - 1 + NZ - 1 + 7)

    own = [lvb.at[0:2, 0, 0:64], lvb.at[2:4, 0, 0:64]]
    sib_own = start(lvb.at[:, 0, 0:64], lvb.at[:, 0, 64:128], at_res(0, 1))
    from_left = [None, None]
    from_right = [None, None]
    from_left[0] = start(own[0], lvb.at[0:2, 3, 0:64], at_res(1, 0))
    from_right[1] = start(own[1], lvb.at[2:4, 1, 0:64], at_res(3, 0))
    from_left[1] = start(own[1], lvb.at[2:4, 3, 0:64], at_res(1, 0))
    from_right[0] = start(own[0], lvb.at[0:2, 1, 0:64], at_res(3, 0))

    act_came = []
    for q, par in pairs:
        lane8 = lanes((8, 128)) % 64
        unused = jnp.where(lane8 < comp_rank[res_of(q, par), 0], 0.0, 1.0)
        if (q, par) == (0, 0):
            actr[0] = unused
        else:
            act[2 * q + par] = unused
            act_came.append(start(act.at[2 * q + par], actr.at[back[(q, par)]], at_res(q, par)))

    nb = near_block[0, 0]
    for k in range(4):
        mask = row_mask(right_rank[k, 0], (64, 1024))
        rum[k] = ru_ref[k] * mask
        rvm[64 * k : 64 * k + 64, :] = rv_ref[k] * mask
        lum[64 * k : 64 * k + 64, :] = lu_ref[k] * row_mask(left_rank[0, k], (64, 1024))
    omega = omega_ref[...]
    mixed = [dot_nt(omega, rvm[64 * k : 64 * k + 64, :]) for k in range(4)]
    for n in range(4):
        cols = slice(256 * n, 256 * n + 256)
        near_omega = dot_nt(omega, near_ref[cols, :])
        for k in range(4):
            high = mixed[k].astype(BF)
            low = (mixed[k] - high.astype(F32)).astype(BF)
            part = dot_nn(high, rum[k, :, cols]) + dot_nn(low, rum[k, :, cols])
            full = jnp.where(nb == k, near_omega, part)
            high = full.astype(BF)
            wt[k, 0:64, cols] = high
            wt[k, 64:128, cols] = (full - high.astype(F32)).astype(BF)

    def expand_chip(q):
        lane = lanes((64, 128))
        parts = []
        for k in range(4):
            both = dot_nt(wt[k], lvb[k, q])
            parts.append(both[0:64] + both[64:128])
        rolled = [pltpu.roll(part, 64, 1) for part in parts]
        for par in range(2):
            if par == 0:
                tiles = [jnp.where(lane < 64, parts[2 * t], rolled[2 * t + 1]) for t in range(2)]
            else:
                tiles = [jnp.where(lane < 64, rolled[2 * t], parts[2 * t + 1]) for t in range(2)]
            active = row_mask(comp_rank[res_of(q, par), 0], (64, 128))
            for t in range(2):
                value = tiles[t].astype(BF) * active
                if (q, par) == (0, 0):
                    exr[0, :, 128 * t : 128 * t + 128] = value
                else:
                    exs[2 * q + par, :, 128 * t : 128 * t + 128] = value

    came = {}

    def send_expand(q, par):
        slot = back[(q, par)]
        came[slot] = start(exs.at[2 * q + par], exr.at[slot], at_res(q, par))

    sib_own.wait_recv()
    expand_chip(0)
    send_expand(0, 1)

    sibling = at_res(0, 1)
    fwd = {1: [], 2: [], 3: []}
    from_left[0].wait_recv()
    relay_left = start(lvb.at[0:2, 3, 0:64], lvb.at[0:2, 2, 0:64], at_res(1, 0))
    fwd[3].append(start(lvb.at[0:2, 3, 0:64], lvb.at[0:2, 3, 64:128], sibling))
    from_right[1].wait_recv()
    relay_right = start(lvb.at[2:4, 1, 0:64], lvb.at[2:4, 2, 0:64], at_res(3, 0))
    fwd[1].append(start(lvb.at[2:4, 1, 0:64], lvb.at[2:4, 1, 64:128], sibling))
    from_left[1].wait_recv()
    fwd[3].append(start(lvb.at[2:4, 3, 0:64], lvb.at[2:4, 3, 64:128], sibling))
    from_right[0].wait_recv()
    fwd[1].append(start(lvb.at[0:2, 1, 0:64], lvb.at[0:2, 1, 64:128], sibling))
    for q in (3, 1):
        for copy in fwd[q]:
            copy.wait_recv()
        expand_chip(q)
        send_expand(q, 0)
        send_expand(q, 1)
    relay_left.wait_recv()
    fwd[2].append(start(lvb.at[0:2, 2, 0:64], lvb.at[0:2, 2, 64:128], sibling))
    relay_right.wait_recv()
    fwd[2].append(start(lvb.at[2:4, 2, 0:64], lvb.at[2:4, 2, 64:128], sibling))
    for copy in fwd[2]:
        copy.wait_recv()
    expand_chip(2)
    send_expand(2, 0)
    send_expand(2, 1)

    for q in (0, 3, 1, 2):
        for par in range(2):
            if (q, par) != (0, 0):
                came[2 * q + par].wait_recv()
        factor = exr[2 * q : 2 * q + 2].reshape(128, 256)
        for n in range(4):
            part = dot_nn(factor, lum[:, 256 * n : 256 * n + 256]).astype(BF)
            for par in range(2):
                ska[2 * q + par, :, 256 * n : 256 * n + 256] = part[64 * par : 64 * par + 32]
                for t in range(2):
                    skb[2 * n + t, 2 * q + par] = part[64 * par + 32 : 64 * par + 64, 128 * t : 128 * t + 128]

    def slot_of(column):
        return lax.rem(column // 2 - x + NX, NX) * 2 + lax.rem(column + c, 2)

    got_a, got_b = [], []
    for d in range(1, 8):
        got_a.append(start(ska.at[slot_of(lax.rem(y + d, NY))], ra.at[d - 1], at_y(d)))
        got_b.append(start(skb.at[lax.rem(z + d, NZ)], rb.at[d - 1], at_z(d)))

    for k in range(4):
        for q in range(NX):
            kept = jnp.where(nb == k, lvb[k, q], lvsel[128 * q : 128 * q + 128, :] if k else jnp.zeros((128, 1024), BF))
            lvsel[128 * q : 128 * q + 128, :] = kept

    def weights(n, carry):
        cols = pl.ds(pl.multiple_of(n * 256, 256), 256)
        tile = near_ref[:, cols]
        for q in range(NX):
            near_part = dot_nn(lvsel[128 * q : 128 * q + 128, :], tile)
            for k in range(4):
                far_part = dot_nn(held[k, 128 * q : 128 * q + 128, 0:64], rvm[64 * k : 64 * k + 64, cols])
                value = jnp.where(nb == k, near_part, far_part).astype(BF)
                wgt[2 * q, 64 * k : 64 * k + 64, cols] = value[0:64]
                wgt[2 * q + 1, 64 * k : 64 * k + 64, cols] = value[64:128]
        return carry

    for k in range(4):
        for q in range(NX):
            held[k, 128 * q : 128 * q + 128, 0:64] = dot_nt(lvb[k, q], rum[k]).astype(BF)
    lax.fori_loop(0, 4, weights, 0)

    for copy in got_a:
        copy.wait_recv()
    mine = slot_of(y)
    for n in range(8):
        cols = slice(128 * n, 128 * n + 128)
        total = ska[mine, :, cols].astype(F32)
        for d in range(7):
            total = total + ra[d, :, cols].astype(F32)
        sa[n] = total
    got_a = [start(sa.at[lax.rem(z + d, NZ)], ra2.at[d - 1], at_z(d)) for d in range(1, 8)]
    for copy in got_b:
        copy.wait_recv()
    for n in range(8):
        total = skb[z, n].astype(F32)
        for d in range(7):
            total = total + rb[d, n].astype(F32)
        sb[n] = total
    got_b = [start(sb.at[slot_of(lax.rem(y + d, NY))], rb2.at[d - 1], at_y(d)) for d in range(1, 8)]
    for copy in got_a + got_b:
        copy.wait_recv()
    low_half = sa[z]
    high_half = sb[mine]
    for d in range(7):
        low_half = low_half + ra2[d]
        high_half = high_half + rb2[d]

    zcols = pl.ds(pl.multiple_of(z * 128, 128), 128)
    sfull[y, 0:32, zcols] = low_half.astype(BF)
    sfull[y, 32:64, zcols] = high_half.astype(BF)
    got_a, got_b = [], []
    for d in range(1, 8):
        got_a.append(start(sfull.at[y, 0:32, zcols], sfull.at[y, 0:32, zcols], at_z(d)))
        got_b.append(start(sfull.at[y, 32:64, zcols], sfull.at[y, 32:64, zcols], at_y(d)))

    part = jnp.concatenate([low_half, high_half], axis=0)
    twice = jnp.concatenate([part, part], axis=0)
    gram = dot_nt(part, twice, HIGHEST)
    gs[...] = jnp.where(lanes((32, 128)) < 64, gram[0:32], gram[32:64])
    got_gram = [start(gs, gr.at[d - 1], at_z(d)) for d in range(1, 8)]

    for copy in got_a:
        copy.wait_recv()
    got_a = [start(sfull.at[y, 0:32], sfull.at[y, 0:32], at_y(d)) for d in range(1, 8)]
    for copy in got_b:
        copy.wait_recv()
    got_b = [start(sfull.at[:, 32:64, zcols], sfull.at[:, 32:64, zcols], at_z(d)) for d in range(1, 8)]

    for copy in got_gram:
        copy.wait_recv()
    total = gs[...]
    for d in range(7):
        total = total + gr[d]
    lane32 = lanes((32, 128))
    rows32 = lax.broadcasted_iota(jnp.int32, (32, 128), 0)
    index = jnp.where(lane32 < 64, rows32, rows32 + 32)
    for copy in act_came:
        copy.wait_recv()
    unused = jnp.where(lane32 % 64 == index, actr[mine, 0:1, :], 0.0)
    linvg[y] = inverse_factor(total + unused)
    got_inverse = [start(linvg.at[y], linvg.at[y], at_y(d)) for d in range(1, 8)]

    for copy in got_a + got_b:
        copy.wait_recv()

    for j in range(0, 8, 2):
        value = dot_nt(sfull[j : j + 2].reshape(128, 1024), lum[...]).astype(BF)
        ut[j] = value[0:64]
        ut[j + 1] = value[64:128]
    came = {}
    for q, par in others:
        came[back[(q, par)]] = start(ut.at[res_of(q, par)], utr.at[back[(q, par)]], at_res(q, par))
    utr[0] = ut[r]
    row_cols = pl.ds(pl.multiple_of(y * 128, 128), 128)
    rows_came = []
    for q, par in others:
        rows_came.append(start(sfull.at[res_of(q, par), :, row_cols], srr.at[back[(q, par)]], at_res(q, par)))
    srr[0] = sfull[r, :, row_cols]
    for copy in got_inverse:
        copy.wait_recv()
    inverse_came = []
    for q, par in others:
        inverse_came.append(start(linvg.at[res_of(q, par)], linvr.at[back[(q, par)]], at_res(q, par)))
    linvr[0] = linvg[r]

    got_a, got_b = [], []
    for slot in (0, 1, 6, 7, 2, 3, 4, 5):
        if slot:
            came[slot].wait_recv()
        factor = utr[slot]
        for n in range(4):
            part = dot_nn(factor, wgt[slot, :, 256 * n : 256 * n + 256])
            for t in range(2):
                tile = part[:, 128 * t : 128 * t + 128]
                if slot < 4:
                    ia[2 * n + t, 64 * slot : 64 * slot + 64, :] = tile.astype(BF)
                else:
                    imt[2 * n + t, 64 * (slot - 4) : 64 * (slot - 4) + 64, :] = tile
        if slot == 3:
            for d in range(1, 8):
                got_a.append(start(ia.at[lax.rem(y + d, NY)], ria.at[d - 1], at_y(d)))
    for n in range(8):
        ib[:, n] = imt[n].T.astype(BF).reshape(8, 16, 256)
    for d in range(1, 8):
        got_b.append(start(ib.at[lax.rem(z + d, NZ)], rib.at[d - 1], at_z(d)))

    for copy in got_a:
        copy.wait_recv()
    total = ia[y].astype(F32)
    for d in range(7):
        total = total + ria[d].astype(F32)
    fa[...] = total.T.reshape(8, 16, 256)
    got_a = [start(fa.at[lax.rem(z + d, NZ)], ria2.at[d - 1], at_z(d)) for d in range(1, 8)]
    for copy in got_b:
        copy.wait_recv()
    for n in range(8):
        total = ib[z, n].astype(F32)
        for d in range(7):
            total = total + rib[d, n].astype(F32)
        fb[n] = total
    got_b = [start(fb.at[lax.rem(y + d, NY)], rib2.at[d - 1], at_y(d)) for d in range(1, 8)]

    for copy in rows_came + inverse_came:
        copy.wait_recv()
    both = []
    for t in range(NX):
        factor = block_pair(linvr[2 * t], linvr[2 * t + 1])
        both.append(factor)
        turned = dot_nn(factor, srr[2 * t : 2 * t + 2].reshape(128, 128).astype(F32), HIGHEST).T
        rows[...] = turned.reshape(8, 16, 128)
        value = rows[z]
        basis_ref[res_of(t, 0)] = value[:, 0:64]
        basis_ref[res_of(t, 1)] = pltpu.roll(value, 64, 1)[:, 0:64]
    for copy in got_a + got_b:
        copy.wait_recv()
    first, second = fa[z], fb[y]
    for d in range(7):
        first = first + ria2[d]
        second = second + rib2[d]
    for t in range(NX):
        half = first if t < 2 else second
        value = dot_nt(half[:, 128 * (t % 2) : 128 * (t % 2) + 128], both[t], HIGHEST)
        image_ref[res_of(t, 0)] = value[:, 0:64]
        image_ref[res_of(t, 1)] = pltpu.roll(value, 64, 1)[:, 0:64]
    for copy in pending:
        copy.wait_send()


def local(
    left_u,
    left_v,
    left_rank,
    right_u,
    right_v,
    right_rank,
    near_tiles,
    near_block,
    comp_rank,
    omega,
):
    vmem = pl.BlockSpec(memory_space=pltpu.VMEM)
    smem = pl.BlockSpec(memory_space=pltpu.SMEM)
    scratch = [
        ((4, 4, 128, 1024), BF),
        ((4, 128, 1024), BF),
        ((256, 1024), BF),
        ((4, 64, 1024), BF),
        ((256, 1024), BF),
        ((8, 64, 256), BF),
        ((8, 64, 256), BF),
        ((8, 32, 1024), BF),
        ((8, 8, 32, 128), BF),
        ((7, 32, 1024), BF),
        ((7, 8, 32, 128), BF),
        ((8, 32, 128), F32),
        ((8, 32, 128), F32),
        ((7, 32, 128), F32),
        ((7, 32, 128), F32),
        ((8, 64, 1024), BF),
        ((32, 128), F32),
        ((7, 32, 128), F32),
        ((8, 32, 128), F32),
        ((8, 32, 128), F32),
        ((8, 64, 128), BF),
        ((8, 64, 256), BF),
        ((8, 64, 256), BF),
        ((512, 1024), BF),
        ((4, 512, 64), BF),
        ((8, 256, 1024), BF),
        ((8, 8, 128), F32),
        ((8, 8, 128), F32),
        ((8, 256, 128), BF),
        ((8, 8, 16, 256), BF),
        ((8, 256, 128), F32),
        ((7, 256, 128), BF),
        ((7, 8, 16, 256), BF),
        ((8, 16, 256), F32),
        ((8, 16, 256), F32),
        ((7, 16, 256), F32),
        ((7, 16, 256), F32),
        ((8, 16, 128), F32),
    ]
    basis, image = pl.pallas_call(
        kernel,
        out_shape=[jax.ShapeDtypeStruct((8, 16, 64), F32)] * 2,
        in_specs=[vmem] * 6 + [smem] * 4,
        out_specs=[vmem, vmem],
        scratch_shapes=[pltpu.VMEM(shape, dtype) for shape, dtype in scratch]
        + [pltpu.SemaphoreType.DMA((COPIES,)), pltpu.SemaphoreType.DMA((COPIES,))],
        compiler_params=pltpu.CompilerParams(
            collective_id=0, has_side_effects=True, vmem_limit_bytes=50 * 1024 * 1024
        ),
    )(
        jnp.swapaxes(left_v[0], 1, 2),
        jnp.swapaxes(left_u[0], 1, 2),
        jnp.swapaxes(right_u[:, 0], 1, 2),
        jnp.swapaxes(right_v[:, 0], 1, 2),
        near_tiles[0, 0],
        jnp.swapaxes(omega[0], 0, 1),
        left_rank,
        right_rank,
        near_block,
        comp_rank,
    )
    return basis[:, None], image[:, None]


def solution(mesh):
    placed = (
        P("res", "inner", None, None),
        P("res", "inner", None, None),
        P("res", "inner"),
        P("inner", "res", None, None),
        P("inner", "res", None, None),
        P("inner", "res"),
        P("inner", "res", None, None),
        P("inner", "res"),
        P(None, "res"),
        P("res", None, None),
    )
    return jax.shard_map(
        local,
        mesh=mesh,
        in_specs=placed,
        out_specs=(P(None, "res", "inner", None), P(None, "res", "inner", None)),
        check_vma=False,
    )
```

time: 623 us -> 121 us (0.19)
  waiting for transfers between devices: 454 us -> 0 us
  Pallas kernels: 0 us -> 111 us
  other arithmetic: 90.7 us -> 0 us
  matrix products: 37.5 us -> 0 us
  blocking collectives: 14.7 us -> 0 us
  between operations: 14.6 us -> 1.29 us
    reduce_scatter x1 -> x0, waiting for transfers between devices: 241 us -> none  [local(): lax.psum_scatter(jnp.einsum('ikjcr,ikjrs->cijs', weight, projected, prefe...]
    psum x1 -> x0, waiting for transfers between devices: 159 us -> none  [compress(): sketch = lax.psum(partial_value, 'inner')]
    pallas_call x0 -> x1, Pallas kernels: none -> 111 us  [local(): pl.pallas_call(kernel, out_shape=[jax.ShapeDtypeStruct((8, 16, 64), F32)]...]
    another operation x7 -> x0, other arithmetic: 86.5 us -> none  [the longest x4 47.1 us: compress(): lower_factor = jnp.linalg.cholesky(gram_of(sketch) + unused)]
    all_gather x2 -> x0, waiting for transfers between devices: 52.8 us -> none  [the longest x1 28 us: local(): lax.all_gather(left_v, 'res', axis=0, tiled=True)]
    dot_general x6 -> x0, matrix products: 32.6 us -> none  [the longest x1 8.34 us: local(): jnp.einsum('ikjcr,ikjrs->cijs', weight, projected, preferred_element_type...]
    all_gather x1 -> x0, blocking collectives: 14.7 us -> none  [local(): lax.all_gather(left_rank, 'res', axis=0, tiled=True)]
    unnamed x13 -> x16, local copies, waits for them, and re-layouts: 1.52 us -> 8.45 us
  transfers between devices with their start and end apart: 4 -> 0, of which waited for: 4 -> 0; matrix products, arithmetic and copies ran while one was open for 3% -> 0% of each run, Pallas kernels for 0% -> 0%
where the time goes in v1:
time: 121 us
  Pallas kernels  111 us (92%)
  local copies, waits for them, and re-layouts  8.45 us (7%)
  between operations  1.29 us (1%)
    pallas_call x1, Pallas kernels, local(): pl.pallas_call(kernel, out_shape=[jax.ShapeDtypeStruct((8, 16, 64), F32)]...  111 us
    unnamed x16, local copies, waits for them, and re-layouts  8.45 us

profile of v1, /device:TPU:1, one launch (start us, length us, event | category | flops | bytes accessed | tf_op | source)
XLA Modules:
  0.0 120.6 jit_solution(8362339118701820964)
XLA Ops:
  1.3 0.7 copy.12.right_rank
  2.0 0.7 copy.13.comp_rank
  2.7 0.0 copy-start
  2.8 1.0 copy-done
  3.8 0.0 copy-start.1
  3.8 1.0 copy-done.1
  4.8 0.0 copy-start.2
  4.8 1.0 copy-done.2
  5.9 0.0 copy-start.3
  5.9 1.0 copy-done.3
  6.9 0.0 copy-start.4
  6.9 0.9 copy-done.4
  7.8 0.0 copy-start.5
  7.8 0.7 copy-done.5
  8.5 110.8 %shard_map.113 = (f32[8,16,64]{2,1,0:T(8,128)S(1)}, f32[8,16,64]{2,1,0:T(8,128)S(1)}) custom-call(bf16[4,64,1024]{2,1,0:T(8,128)(2,1)S(1)} %bitcast.22, bf16[4,64,1024]{2,1,0:T(8,128)(2,1)S(1)} %bitcast.23, bf16[4,64,1024]{2,1,0:T(8,128)(2,1)S(1)} %bitcast.24, bf16[4,64,1024]{2,1,0:T(8,128)(2,1)S(1)} %bitcast.25, bf16[1024,1024]{1,0:T(8,128)(2,1)} %bitcast.29, ...), custom_call_target="tpu_custom_call" | custom-call | tf_op jit(solution)/shard_map/pallas_call | solution.py:519
  119.3 0.6 copy.19
  120.0 0.6 copy.20
Async XLA Ops:
  2.7 1.0 copy-start
  3.8 1.0 copy-start.1
  4.8 1.0 copy-start.2
  5.9 1.0 copy-start.3
  6.9 0.9 copy-start.4
  7.8 0.7 copy-start.5

commit v2 on v1

--- a/solution.py
+++ b/solution.py
@@ -12,7 +12,7 @@
 NY = 8
 NZ = 8
 NX = 4
-COPIES = 160
+COPIES = 180
 
 
 def dot_nn(a, b, precision=None):
@@ -32,29 +32,37 @@
     return jnp.where(rows < rank, 1.0, 0.0).astype(BF)
 
 
-def inverse_factor(gram):
+def unpack_with_identity(gram):
     lane32 = lanes((32, 128))
     rows32 = lax.broadcasted_iota(jnp.int32, (32, 128), 0)
     top = jnp.where(lane32 < 64, gram, jnp.where(lane32 - 64 == rows32, 1.0, 0.0))
     bottom = jnp.where(lane32 < 64, pltpu.roll(gram, 64, 1), jnp.where(lane32 - 96 == rows32, 1.0, 0.0))
-    blocks = [top[8 * b : 8 * b + 8] for b in range(4)] + [bottom[8 * b : 8 * b + 8] for b in range(4)]
+    return [top[8 * b : 8 * b + 8] for b in range(4)] + [bottom[8 * b : 8 * b + 8] for b in range(4)]
+
+
+def eliminate(blocks, first, last):
     rows8 = lax.broadcasted_iota(jnp.int32, (8, 128), 0)
-    for k in range(64):
+    for k in range(first, last):
         kb, kr = k // 8, k % 8
         row = blocks[kb][kr : kr + 1, :]
         scaled = row / row[:, k : k + 1]
         for b in range(kb, 8):
-            factor = blocks[b][:, k : k + 1]
-            update = factor * scaled
+            update = blocks[b][:, k : k + 1] * scaled
             if b == kb:
                 update = jnp.where(rows8 > kr, update, 0.0)
             blocks[b] = blocks[b] - update
+
+
+def inverse_of(blocks):
     lane8 = lanes((8, 128))
+    lane32 = lanes((32, 128))
+    rows8 = lax.broadcasted_iota(jnp.int32, (8, 128), 0)
+    scaled = []
     for b in range(8):
         diagonal = jnp.sum(jnp.where(lane8 == rows8 + 8 * b, blocks[b], 0.0), axis=1, keepdims=True)
-        blocks[b] = blocks[b] * (1.0 / jnp.sqrt(diagonal))
-    top = jnp.concatenate(blocks[:4], axis=0)
-    bottom = jnp.concatenate(blocks[4:], axis=0)
+        scaled.append(blocks[b] * (1.0 / jnp.sqrt(diagonal)))
+    top = jnp.concatenate(scaled[:4], axis=0)
+    bottom = jnp.concatenate(scaled[4:], axis=0)
     return jnp.where(lane32 < 64, pltpu.roll(top, 64, 1), bottom)
 
 
@@ -73,18 +81,24 @@
 
 
 def kernel(
+    lv_hbm,
+    lu_hbm,
+    ru_hbm,
+    rv_hbm,
+    near_hbm,
+    omega_hbm,
+    left_rank,
+    right_rank,
+    near_block,
+    comp_rank,
+    basis_ref,
+    image_ref,
     lv_ref,
     lu_ref,
     ru_ref,
     rv_ref,
     near_ref,
     omega_ref,
-    left_rank,
-    right_rank,
-    near_block,
-    comp_rank,
-    basis_ref,
-    image_ref,
     lvb,
     wt,
     lum,
@@ -115,7 +129,6 @@
     actr,
     ia,
     ib,
-    imt,
     ria,
     rib,
     fa,
@@ -123,6 +136,7 @@
     ria2,
     rib2,
     rows,
+    load_sem,
     send_sem,
     recv_sem,
 ):
@@ -131,6 +145,17 @@
     y, z = p // NZ, p % NZ
     x, c = r // 2, r % 2
     used = [0]
+    moves = (
+        (lv_hbm, lv_ref),
+        (rv_hbm, rv_ref),
+        (omega_hbm, omega_ref),
+        (ru_hbm, ru_ref),
+        (near_hbm, near_ref),
+        (lu_hbm, lu_ref),
+    )
+    loads = [pltpu.make_async_copy(src, dst, load_sem.at[n]) for n, (src, dst) in enumerate(moves)]
+    for load in loads:
+        load.start()
 
     def at_y(d):
         return (lax.rem(y + d, NY) * NZ + z, r)
@@ -160,6 +185,21 @@
         return copy
 
     pending = []
+
+    def start_unless_own(distance, src, lands, base, device):
+        n = lax.rem(distance + 7, 8)
+
+        @pl.when(distance != 0)
+        def _():
+            pltpu.make_async_remote_copy(
+                src_ref=src,
+                dst_ref=lands.at[n],
+                send_sem=send_sem.at[base + n],
+                recv_sem=recv_sem.at[base + n],
+                device_id=device,
+                device_id_type=MESH,
+            ).start()
+
     pairs = [(q, par) for q in range(NX) for par in range(2)]
     others = pairs[1:]
     back = {(q, par): ((NX - q) % NX) * 2 + par for q, par in pairs}
@@ -172,32 +212,60 @@
     for q, par in others:
         pl.semaphore_signal(barrier, inc=1, device_id=at_res(q, par), device_id_type=MESH)
 
+    loads[0].wait()
     for k in range(4):
         lvb[k, 0, 0:64, :] = lv_ref[k] * row_mask(left_rank[0, k], (64, 1024))
     pl.semaphore_wait(barrier, NY - 1 + NZ - 1 + 7)
 
-    own = [lvb.at[0:2, 0, 0:64], lvb.at[2:4, 0, 0:64]]
-    sib_own = start(lvb.at[:, 0, 0:64], lvb.at[:, 0, 64:128], at_res(0, 1))
-    from_left = [None, None]
-    from_right = [None, None]
-    from_left[0] = start(own[0], lvb.at[0:2, 3, 0:64], at_res(1, 0))
-    from_right[1] = start(own[1], lvb.at[2:4, 1, 0:64], at_res(3, 0))
-    from_left[1] = start(own[1], lvb.at[2:4, 3, 0:64], at_res(1, 0))
-    from_right[0] = start(own[0], lvb.at[0:2, 1, 0:64], at_res(3, 0))
+    nb = near_block[0, 0]
+
+    def pick_near(q):
+        rows = slice(128 * q, 128 * q + 128)
+        kept = jnp.zeros((128, 1024), BF)
+        for k in range(4):
+            kept = jnp.where(nb == k, lvb[k, q], kept)
+            held[k, rows, :] = dot_nt(lvb[k, q], rum[k]).astype(BF)
+        lvsel[rows, :] = kept
+
+    def make_weights(n):
+        cols = slice(256 * n, 256 * n + 256)
+        tile = near_ref[:, cols]
+        for q in range(NX):
+            rows = slice(128 * q, 128 * q + 128)
+            near_part = dot_nn(lvsel[rows, :], tile)
+            for k in range(4):
+                far_part = dot_nn(held[k, rows, :], rvm[64 * k : 64 * k + 64, cols])
+                value = jnp.where(nb == k, near_part, far_part).astype(BF)
+                wgt[2 * q, 64 * k : 64 * k + 64, cols] = value[0:64]
+                wgt[2 * q + 1, 64 * k : 64 * k + 64, cols] = value[64:128]
+
+    def piece_of(step, n):
+        return lambda: step(n)
+
+    weight_work = [piece_of(pick_near, q) for q in range(4)] + [piece_of(make_weights, n) for n in range(4)]
+
+    halves = (slice(0, 2), slice(2, 4))
+    sibling = at_res(0, 1)
+    sib_own = start(lvb.at[:, 0, 0:64], lvb.at[:, 0, 64:128], sibling)
+    came_v = {}
+    for half in halves:
+        came_v[3, half.start] = start(lvb.at[half, 0, 0:64], lvb.at[half, 3, 0:64], at_res(1, 0))
+        came_v[1, half.start] = start(lvb.at[half, 0, 0:64], lvb.at[half, 1, 0:64], at_res(3, 0))
 
     act_came = []
     for q, par in pairs:
         lane8 = lanes((8, 128)) % 64
-        unused = jnp.where(lane8 < comp_rank[res_of(q, par), 0], 0.0, 1.0)
+        unused = jnp.where(lane8 < comp_rank[0, res_of(q, par)], 0.0, 1.0)
         if (q, par) == (0, 0):
             actr[0] = unused
         else:
             act[2 * q + par] = unused
             act_came.append(start(act.at[2 * q + par], actr.at[back[(q, par)]], at_res(q, par)))
 
-    nb = near_block[0, 0]
+    for load in loads[1:]:
+        load.wait()
     for k in range(4):
-        mask = row_mask(right_rank[k, 0], (64, 1024))
+        mask = row_mask(right_rank[0, k], (64, 1024))
         rum[k] = ru_ref[k] * mask
         rvm[64 * k : 64 * k + 64, :] = rv_ref[k] * mask
         lum[64 * k : 64 * k + 64, :] = lu_ref[k] * row_mask(left_rank[0, k], (64, 1024))
@@ -227,7 +295,7 @@
                 tiles = [jnp.where(lane < 64, parts[2 * t], rolled[2 * t + 1]) for t in range(2)]
             else:
                 tiles = [jnp.where(lane < 64, rolled[2 * t], parts[2 * t + 1]) for t in range(2)]
-            active = row_mask(comp_rank[res_of(q, par), 0], (64, 128))
+            active = row_mask(comp_rank[0, res_of(q, par)], (64, 128))
             for t in range(2):
                 value = tiles[t].astype(BF) * active
                 if (q, par) == (0, 0):
@@ -241,39 +309,31 @@
         slot = back[(q, par)]
         came[slot] = start(exs.at[2 * q + par], exr.at[slot], at_res(q, par))
 
+    for half in halves:
+        came_v[2, half.start] = start(lvb.at[half, 0, 0:64], lvb.at[half, 2, 0:64], at_res(2, 0))
     sib_own.wait_recv()
     expand_chip(0)
     send_expand(0, 1)
 
-    sibling = at_res(0, 1)
     fwd = {1: [], 2: [], 3: []}
-    from_left[0].wait_recv()
-    relay_left = start(lvb.at[0:2, 3, 0:64], lvb.at[0:2, 2, 0:64], at_res(1, 0))
-    fwd[3].append(start(lvb.at[0:2, 3, 0:64], lvb.at[0:2, 3, 64:128], sibling))
-    from_right[1].wait_recv()
-    relay_right = start(lvb.at[2:4, 1, 0:64], lvb.at[2:4, 2, 0:64], at_res(3, 0))
-    fwd[1].append(start(lvb.at[2:4, 1, 0:64], lvb.at[2:4, 1, 64:128], sibling))
-    from_left[1].wait_recv()
-    fwd[3].append(start(lvb.at[2:4, 3, 0:64], lvb.at[2:4, 3, 64:128], sibling))
-    from_right[0].wait_recv()
-    fwd[1].append(start(lvb.at[0:2, 1, 0:64], lvb.at[0:2, 1, 64:128], sibling))
-    for q in (3, 1):
+
+    def forward(q, half):
+        came_v[q, half.start].wait_recv()
+        fwd[q].append(start(lvb.at[half, q, 0:64], lvb.at[half, q, 64:128], sibling))
+
+    def expand_and_send(q):
         for copy in fwd[q]:
             copy.wait_recv()
         expand_chip(q)
         send_expand(q, 0)
         send_expand(q, 1)
-    relay_left.wait_recv()
-    fwd[2].append(start(lvb.at[0:2, 2, 0:64], lvb.at[0:2, 2, 64:128], sibling))
-    relay_right.wait_recv()
-    fwd[2].append(start(lvb.at[2:4, 2, 0:64], lvb.at[2:4, 2, 64:128], sibling))
-    for copy in fwd[2]:
-        copy.wait_recv()
-    expand_chip(2)
-    send_expand(2, 0)
-    send_expand(2, 1)
-
-    for q in (0, 3, 1, 2):
+
+    def slot_of(column):
+        return lax.rem(column // 2 - x + NX, NX) * 2 + lax.rem(column + c, 2)
+
+    place = {0: 0, 3: 1, 1: 2, 2: 3}
+
+    def sketch_chip(q):
         for par in range(2):
             if (q, par) != (0, 0):
                 came[2 * q + par].wait_recv()
@@ -283,38 +343,50 @@
             for par in range(2):
                 ska[2 * q + par, :, 256 * n : 256 * n + 256] = part[64 * par : 64 * par + 32]
                 for t in range(2):
-                    skb[2 * n + t, 2 * q + par] = part[64 * par + 32 : 64 * par + 64, 128 * t : 128 * t + 128]
-
-    def slot_of(column):
-        return lax.rem(column // 2 - x + NX, NX) * 2 + lax.rem(column + c, 2)
-
-    got_a, got_b = [], []
-    for d in range(1, 8):
-        got_a.append(start(ska.at[slot_of(lax.rem(y + d, NY))], ra.at[d - 1], at_y(d)))
-        got_b.append(start(skb.at[lax.rem(z + d, NZ)], rb.at[d - 1], at_z(d)))
-
-    for k in range(4):
-        for q in range(NX):
-            kept = jnp.where(nb == k, lvb[k, q], lvsel[128 * q : 128 * q + 128, :] if k else jnp.zeros((128, 1024), BF))
-            lvsel[128 * q : 128 * q + 128, :] = kept
-
-    def weights(n, carry):
-        cols = pl.ds(pl.multiple_of(n * 256, 256), 256)
-        tile = near_ref[:, cols]
-        for q in range(NX):
-            near_part = dot_nn(lvsel[128 * q : 128 * q + 128, :], tile)
-            for k in range(4):
-                far_part = dot_nn(held[k, 128 * q : 128 * q + 128, 0:64], rvm[64 * k : 64 * k + 64, cols])
-                value = jnp.where(nb == k, near_part, far_part).astype(BF)
-                wgt[2 * q, 64 * k : 64 * k + 64, cols] = value[0:64]
-                wgt[2 * q + 1, 64 * k : 64 * k + 64, cols] = value[64:128]
-        return carry
-
-    for k in range(4):
-        for q in range(NX):
-            held[k, 128 * q : 128 * q + 128, 0:64] = dot_nt(lvb[k, q], rum[k]).astype(BF)
-    lax.fori_loop(0, 4, weights, 0)
-
+                    tile = part[64 * par + 32 : 64 * par + 64, 128 * t : 128 * t + 128]
+                    skb[2 * n + t, 2 * place[q] + par] = tile
+        for par in range(2):
+            column = res_of(q, par)
+            distance = lax.rem(column - y + NY, NY)
+            start_unless_own(distance, ska.at[2 * q + par], ra, sums_base, (column * NZ + z, r))
+
+    got_b = []
+
+    def send_high(tiles):
+        for d in range(1, NZ):
+            got_b.append(start(skb.at[lax.rem(z + d, NZ), tiles], rb.at[d - 1, tiles], at_z(d)))
+
+    sums_base = used[0]
+    used[0] += 7
+    got_a = []
+    for d in range(7):
+        got_a.append(
+            pltpu.make_async_remote_copy(
+                src_ref=ska.at[0],
+                dst_ref=ra.at[d],
+                send_sem=send_sem.at[sums_base + d],
+                recv_sem=recv_sem.at[sums_base + d],
+                device_id=at_y(d + 1),
+                device_id_type=MESH,
+            )
+        )
+    pending.extend(got_a)
+    for half in halves:
+        forward(3, half)
+        forward(1, half)
+    expand_and_send(3)
+    expand_and_send(1)
+    sketch_chip(0)
+    for half in halves:
+        forward(2, half)
+    expand_and_send(2)
+    sketch_chip(3)
+    sketch_chip(1)
+    send_high(slice(0, 6))
+    sketch_chip(2)
+    send_high(slice(6, 8))
+    for piece in weight_work:
+        piece()
     for copy in got_a:
         copy.wait_recv()
     mine = slot_of(y)
@@ -327,11 +399,12 @@
     got_a = [start(sa.at[lax.rem(z + d, NZ)], ra2.at[d - 1], at_z(d)) for d in range(1, 8)]
     for copy in got_b:
         copy.wait_recv()
-    for n in range(8):
+    for q, par in pairs:
+        n = 2 * place[q] + par
         total = skb[z, n].astype(F32)
         for d in range(7):
             total = total + rb[d, n].astype(F32)
-        sb[n] = total
+        sb[2 * q + par] = total
     got_b = [start(sb.at[slot_of(lax.rem(y + d, NY))], rb2.at[d - 1], at_y(d)) for d in range(1, 8)]
     for copy in got_a + got_b:
         copy.wait_recv()
@@ -357,26 +430,28 @@
 
     for copy in got_a:
         copy.wait_recv()
-    got_a = [start(sfull.at[y, 0:32], sfull.at[y, 0:32], at_y(d)) for d in range(1, 8)]
+    spread = [start(sfull.at[y, 0:32], sfull.at[y, 0:32], at_y(d)) for d in range(1, 8)]
     for copy in got_b:
         copy.wait_recv()
-    got_b = [start(sfull.at[:, 32:64, zcols], sfull.at[:, 32:64, zcols], at_z(d)) for d in range(1, 8)]
-
-    for copy in got_gram:
-        copy.wait_recv()
-    total = gs[...]
-    for d in range(7):
-        total = total + gr[d]
-    lane32 = lanes((32, 128))
-    rows32 = lax.broadcasted_iota(jnp.int32, (32, 128), 0)
-    index = jnp.where(lane32 < 64, rows32, rows32 + 32)
-    for copy in act_came:
-        copy.wait_recv()
-    unused = jnp.where(lane32 % 64 == index, actr[mine, 0:1, :], 0.0)
-    linvg[y] = inverse_factor(total + unused)
-    got_inverse = [start(linvg.at[y], linvg.at[y], at_y(d)) for d in range(1, 8)]
-
-    for copy in got_a + got_b:
+    spread += [start(sfull.at[:, 32:64, zcols], sfull.at[:, 32:64, zcols], at_z(d)) for d in range(1, 8)]
+
+    blocks = []
+
+    def sum_gram():
+        for copy in got_gram + act_came:
+            copy.wait_recv()
+        total = gs[...]
+        for d in range(7):
+            total = total + gr[d]
+        lane32 = lanes((32, 128))
+        rows32 = lax.broadcasted_iota(jnp.int32, (32, 128), 0)
+        index = jnp.where(lane32 < 64, rows32, rows32 + 32)
+        unused = jnp.where(lane32 % 64 == index, actr[mine, 0:1, :], 0.0)
+        blocks.extend(unpack_with_identity(total + unused))
+
+    sum_gram()
+    eliminate(blocks, 0, 40)
+    for copy in spread:
         copy.wait_recv()
 
     for j in range(0, 8, 2):
@@ -392,34 +467,38 @@
     for q, par in others:
         rows_came.append(start(sfull.at[res_of(q, par), :, row_cols], srr.at[back[(q, par)]], at_res(q, par)))
     srr[0] = sfull[r, :, row_cols]
+    eliminate(blocks, 40, 64)
+    linvg[y] = inverse_of(blocks)
+    got_inverse = [start(linvg.at[y], linvg.at[y], at_y(d)) for d in range(1, 8)]
+
+    for slot in range(4):
+        if slot:
+            came[slot].wait_recv()
+        for n in range(4):
+            part = dot_nn(utr[slot], wgt[slot, :, 256 * n : 256 * n + 256])
+            for t in range(2):
+                tile = part[:, 128 * t : 128 * t + 128]
+                ia[2 * n + t, 64 * slot : 64 * slot + 64, :] = tile.astype(BF)
+    got_a = [start(ia.at[lax.rem(y + d, NY)], ria.at[d - 1], at_y(d)) for d in range(1, 8)]
+    for pair in (1, 0):
+        slot = 4 + 2 * pair
+        came[slot].wait_recv()
+        came[slot + 1].wait_recv()
+        for n in range(4):
+            cols = slice(256 * n, 256 * n + 256)
+            part = jnp.concatenate(
+                [dot_nn(utr[slot], wgt[slot, :, cols]), dot_nn(utr[slot + 1], wgt[slot + 1, :, cols])], axis=0
+            )
+            for t in range(2):
+                turned = part[:, 128 * t : 128 * t + 128].T.astype(BF)
+                ib[:, 2 * n + t, :, 128 * pair : 128 * pair + 128] = turned.reshape(8, 16, 128)
+    got_b = [start(ib.at[lax.rem(z + d, NZ)], rib.at[d - 1], at_z(d)) for d in range(1, 8)]
     for copy in got_inverse:
         copy.wait_recv()
     inverse_came = []
     for q, par in others:
         inverse_came.append(start(linvg.at[res_of(q, par)], linvr.at[back[(q, par)]], at_res(q, par)))
     linvr[0] = linvg[r]
-
-    got_a, got_b = [], []
-    for slot in (0, 1, 6, 7, 2, 3, 4, 5):
-        if slot:
-            came[slot].wait_recv()
-        factor = utr[slot]
-        for n in range(4):
-            part = dot_nn(factor, wgt[slot, :, 256 * n : 256 * n + 256])
-            for t in range(2):
-                tile = part[:, 128 * t : 128 * t + 128]
-                if slot < 4:
-                    ia[2 * n + t, 64 * slot : 64 * slot + 64, :] = tile.astype(BF)
-                else:
-                    imt[2 * n + t, 64 * (slot - 4) : 64 * (slot - 4) + 64, :] = tile
-        if slot == 3:
-            for d in range(1, 8):
-                got_a.append(start(ia.at[lax.rem(y + d, NY)], ria.at[d - 1], at_y(d)))
-    for n in range(8):
-        ib[:, n] = imt[n].T.astype(BF).reshape(8, 16, 256)
-    for d in range(1, 8):
-        got_b.append(start(ib.at[lax.rem(z + d, NZ)], rib.at[d - 1], at_z(d)))
-
     for copy in got_a:
         copy.wait_recv()
     total = ia[y].astype(F32)
@@ -477,6 +556,12 @@
     vmem = pl.BlockSpec(memory_space=pltpu.VMEM)
     smem = pl.BlockSpec(memory_space=pltpu.SMEM)
     scratch = [
+        ((4, 64, 1024), BF),
+        ((4, 64, 1024), BF),
+        ((4, 64, 1024), BF),
+        ((4, 64, 1024), BF),
+        ((1024, 1024), BF),
+        ((64, 1024), BF),
         ((4, 4, 128, 1024), BF),
         ((4, 128, 1024), BF),
         ((256, 1024), BF),
@@ -507,7 +592,6 @@
         ((8, 8, 128), F32),
         ((8, 256, 128), BF),
         ((8, 8, 16, 256), BF),
-        ((8, 256, 128), F32),
         ((7, 256, 128), BF),
         ((7, 8, 16, 256), BF),
         ((8, 16, 256), F32),
@@ -519,12 +603,12 @@
     basis, image = pl.pallas_call(
         kernel,
         out_shape=[jax.ShapeDtypeStruct((8, 16, 64), F32)] * 2,
-        in_specs=[vmem] * 6 + [smem] * 4,
+        in_specs=[pl.BlockSpec(memory_space=pl.ANY)] * 6 + [smem] * 4,
         out_specs=[vmem, vmem],
         scratch_shapes=[pltpu.VMEM(shape, dtype) for shape, dtype in scratch]
-        + [pltpu.SemaphoreType.DMA((COPIES,)), pltpu.SemaphoreType.DMA((COPIES,))],
+        + [pltpu.SemaphoreType.DMA((6,)), pltpu.SemaphoreType.DMA((COPIES,)), pltpu.SemaphoreType.DMA((COPIES,))],
         compiler_params=pltpu.CompilerParams(
-            collective_id=0, has_side_effects=True, vmem_limit_bytes=50 * 1024 * 1024
+            collective_id=0, has_side_effects=True, vmem_limit_bytes=60 * 1024 * 1024
         ),
     )(
         jnp.swapaxes(left_v[0], 1, 2),
@@ -534,9 +618,9 @@
         near_tiles[0, 0],
         jnp.swapaxes(omega[0], 0, 1),
         left_rank,
-        right_rank,
+        right_rank.T,
         near_block,
-        comp_rank,
+        comp_rank.T,
     )
     return basis[:, None], image[:, None]
 

time: 121 us -> 120 us (level)
  local copies, waits for them, and re-layouts: 8.45 us -> 2.95 us
  Pallas kernels: 111 us -> 115 us
    unnamed x16 -> x2, local copies, waits for them, and re-layouts: 8.45 us -> 2.95 us
    pallas_call x1, Pallas kernels: 111 us -> 115 us  [local(): pl.pallas_call(kernel, out_shape=[jax.ShapeDtypeStruct((8, 16, 64), F32)]...]
where the time goes in v2:
time: 120 us
  Pallas kernels  115 us (96%)
  local copies, waits for them, and re-layouts  2.95 us (2%)
  between operations  1.29 us (1%)
    pallas_call x1, Pallas kernels, local(): pl.pallas_call(kernel, out_shape=[jax.ShapeDtypeStruct((8, 16, 64), F32)]...  115 us
    unnamed x2, local copies, waits for them, and re-layouts  2.95 us

profile of v2, /device:TPU:1, one launch (start us, length us, event | category | flops | bytes accessed | tf_op | source)
XLA Modules:
  0.0 119.6 jit_solution(13057086009547065483)
XLA Ops:
  1.3 115.4 %shard_map.113 = (f32[8,16,64]{2,1,0:T(8,128)}, f32[8,16,64]{2,1,0:T(8,128)}) custom-call(bf16[4,64,1024]{2,1,0:T(8,128)(2,1)} %bitcast.25, bf16[4,64,1024]{2,1,0:T(8,128)(2,1)} %bitcast.26, bf16[4,64,1024]{2,1,0:T(8,128)(2,1)} %bitcast.27, bf16[4,64,1024]{2,1,0:T(8,128)(2,1)} %bitcast.28, bf16[1024,1024]{1,0:T(8,128)(2,1)} %bitcast.24, ...), custom_call_target="tpu_custom_call" | custom-call | tf_op jit(solution)/shard_map/pallas_call | solution.py:603
  116.7 1.5 %copy.17 = f32[8,1,16,64]{3,2,1,0:T(8,128)} copy(f32[8,1,16,64]{3,2,1,0:T(8,128)} %bitcast.31) | data formatting | bytes 65536
  118.1 1.5 %copy.18 = f32[8,1,16,64]{3,2,1,0:T(8,128)} copy(f32[8,1,16,64]{3,2,1,0:T(8,128)} %bitcast.30) | data formatting | bytes 65536

commit v3 on v2

--- a/solution.py
+++ b/solution.py
@@ -244,13 +244,13 @@
 
     weight_work = [piece_of(pick_near, q) for q in range(4)] + [piece_of(make_weights, n) for n in range(4)]
 
-    halves = (slice(0, 2), slice(2, 4))
     sibling = at_res(0, 1)
     sib_own = start(lvb.at[:, 0, 0:64], lvb.at[:, 0, 64:128], sibling)
     came_v = {}
-    for half in halves:
-        came_v[3, half.start] = start(lvb.at[half, 0, 0:64], lvb.at[half, 3, 0:64], at_res(1, 0))
-        came_v[1, half.start] = start(lvb.at[half, 0, 0:64], lvb.at[half, 1, 0:64], at_res(3, 0))
+    for k in range(4):
+        turned = (k + 2) % 4
+        came_v[3, k] = start(lvb.at[k, 0, 0:64], lvb.at[k, 3, 0:64], at_res(1, 0))
+        came_v[1, turned] = start(lvb.at[turned, 0, 0:64], lvb.at[turned, 1, 0:64], at_res(3, 0))
 
     act_came = []
     for q, par in pairs:
@@ -309,17 +309,19 @@
         slot = back[(q, par)]
         came[slot] = start(exs.at[2 * q + par], exr.at[slot], at_res(q, par))
 
-    for half in halves:
-        came_v[2, half.start] = start(lvb.at[half, 0, 0:64], lvb.at[half, 2, 0:64], at_res(2, 0))
     sib_own.wait_recv()
     expand_chip(0)
     send_expand(0, 1)
 
     fwd = {1: [], 2: [], 3: []}
 
-    def forward(q, half):
-        came_v[q, half.start].wait_recv()
-        fwd[q].append(start(lvb.at[half, q, 0:64], lvb.at[half, q, 64:128], sibling))
+    def forward(q, k):
+        came_v[q, k].wait_recv()
+        if (q, k) in ((3, 0), (3, 1)):
+            came_v[2, k] = start(lvb.at[k, 3, 0:64], lvb.at[k, 2, 0:64], at_res(1, 0))
+        if (q, k) in ((1, 2), (1, 3)):
+            came_v[2, k] = start(lvb.at[k, 1, 0:64], lvb.at[k, 2, 0:64], at_res(3, 0))
+        fwd[q].append(start(lvb.at[k, q, 0:64], lvb.at[k, q, 64:128], sibling))
 
     def expand_and_send(q):
         for copy in fwd[q]:
@@ -371,14 +373,14 @@
             )
         )
     pending.extend(got_a)
-    for half in halves:
-        forward(3, half)
-        forward(1, half)
+    for k in range(4):
+        forward(3, k)
+        forward(1, (k + 2) % 4)
     expand_and_send(3)
     expand_and_send(1)
     sketch_chip(0)
-    for half in halves:
-        forward(2, half)
+    for k in (0, 2, 1, 3):
+        forward(2, k)
     expand_and_send(2)
     sketch_chip(3)
     sketch_chip(1)

time: 120 us -> 115 us (0.958)
  Pallas kernels: 115 us -> 111 us
    pallas_call x1, Pallas kernels: 115 us -> 111 us  [local(): pl.pallas_call(kernel, out_shape=[jax.ShapeDtypeStruct((8, 16, 64), F32)]...]
where the time goes in v3:
time: 115 us
  Pallas kernels  111 us (97%)
  local copies, waits for them, and re-layouts  2.95 us (3%)
  between operations  1.29 us (1%)
    pallas_call x1, Pallas kernels, local(): pl.pallas_call(kernel, out_shape=[jax.ShapeDtypeStruct((8, 16, 64), F32)]...  111 us
    unnamed x2, local copies, waits for them, and re-layouts  2.95 us

profile of v3, /device:TPU:1, one launch (start us, length us, event | category | flops | bytes accessed | tf_op | source)
XLA Modules:
  0.0 114.8 jit_solution(2687730025271748598)
XLA Ops:
  1.3 110.6 %shard_map.113 = (f32[8,16,64]{2,1,0:T(8,128)}, f32[8,16,64]{2,1,0:T(8,128)}) custom-call(bf16[4,64,1024]{2,1,0:T(8,128)(2,1)} %bitcast.25, bf16[4,64,1024]{2,1,0:T(8,128)(2,1)} %bitcast.26, bf16[4,64,1024]{2,1,0:T(8,128)(2,1)} %bitcast.27, bf16[4,64,1024]{2,1,0:T(8,128)(2,1)} %bitcast.28, bf16[1024,1024]{1,0:T(8,128)(2,1)} %bitcast.24, ...), custom_call_target="tpu_custom_call" | custom-call | tf_op jit(solution)/shard_map/pallas_call | solution.py:605
  111.9 1.5 %copy.17 = f32[8,1,16,64]{3,2,1,0:T(8,128)} copy(f32[8,1,16,64]{3,2,1,0:T(8,128)} %bitcast.31) | data formatting | bytes 65536
  113.3 1.5 %copy.18 = f32[8,1,16,64]{3,2,1,0:T(8,128)} copy(f32[8,1,16,64]{3,2,1,0:T(8,128)} %bitcast.30) | data formatting | bytes 65536

commit v4 on v3

--- a/solution.py
+++ b/solution.py
@@ -12,6 +12,7 @@
 NY = 8
 NZ = 8
 NX = 4
+FAR_FIRST = (4, 3, 5, 2, 6, 1, 7)
 COPIES = 180
 
 
@@ -252,6 +253,16 @@
         came_v[3, k] = start(lvb.at[k, 0, 0:64], lvb.at[k, 3, 0:64], at_res(1, 0))
         came_v[1, turned] = start(lvb.at[turned, 0, 0:64], lvb.at[turned, 1, 0:64], at_res(3, 0))
 
+    fwd = {1: [], 2: [], 3: []}
+
+    def forward(q, k):
+        came_v[q, k].wait_recv()
+        if (q, k) in ((3, 0), (3, 1)):
+            came_v[2, k] = start(lvb.at[k, 3, 0:64], lvb.at[k, 2, 0:64], at_res(1, 0))
+        if (q, k) in ((1, 2), (1, 3)):
+            came_v[2, k] = start(lvb.at[k, 1, 0:64], lvb.at[k, 2, 0:64], at_res(3, 0))
+        fwd[q].append(start(lvb.at[k, q, 0:64], lvb.at[k, q, 64:128], sibling))
+
     act_came = []
     for q, par in pairs:
         lane8 = lanes((8, 128)) % 64
@@ -282,6 +293,9 @@
             high = full.astype(BF)
             wt[k, 0:64, cols] = high
             wt[k, 64:128, cols] = (full - high.astype(F32)).astype(BF)
+        if n % 2:
+            forward(3, n // 2)
+            forward(1, n // 2 + 2)
 
     def expand_chip(q):
         lane = lanes((64, 128))
@@ -313,16 +327,6 @@
     expand_chip(0)
     send_expand(0, 1)
 
-    fwd = {1: [], 2: [], 3: []}
-
-    def forward(q, k):
-        came_v[q, k].wait_recv()
-        if (q, k) in ((3, 0), (3, 1)):
-            came_v[2, k] = start(lvb.at[k, 3, 0:64], lvb.at[k, 2, 0:64], at_res(1, 0))
-        if (q, k) in ((1, 2), (1, 3)):
-            came_v[2, k] = start(lvb.at[k, 1, 0:64], lvb.at[k, 2, 0:64], at_res(3, 0))
-        fwd[q].append(start(lvb.at[k, q, 0:64], lvb.at[k, q, 64:128], sibling))
-
     def expand_and_send(q):
         for copy in fwd[q]:
             copy.wait_recv()
@@ -355,7 +359,7 @@
     got_b = []
 
     def send_high(tiles):
-        for d in range(1, NZ):
+        for d in FAR_FIRST:
             got_b.append(start(skb.at[lax.rem(z + d, NZ), tiles], rb.at[d - 1, tiles], at_z(d)))
 
     sums_base = used[0]
@@ -373,9 +377,9 @@
             )
         )
     pending.extend(got_a)
-    for k in range(4):
+    for k in (2, 3):
         forward(3, k)
-        forward(1, (k + 2) % 4)
+        forward(1, k - 2)
     expand_and_send(3)
     expand_and_send(1)
     sketch_chip(0)
@@ -398,7 +402,7 @@
         for d in range(7):
             total = total + ra[d, :, cols].astype(F32)
         sa[n] = total
-    got_a = [start(sa.at[lax.rem(z + d, NZ)], ra2.at[d - 1], at_z(d)) for d in range(1, 8)]
+    got_a = [start(sa.at[lax.rem(z + d, NZ)], ra2.at[d - 1], at_z(d)) for d in FAR_FIRST]
     for copy in got_b:
         copy.wait_recv()
     for q, par in pairs:
@@ -407,7 +411,7 @@
         for d in range(7):
             total = total + rb[d, n].astype(F32)
         sb[2 * q + par] = total
-    got_b = [start(sb.at[slot_of(lax.rem(y + d, NY))], rb2.at[d - 1], at_y(d)) for d in range(1, 8)]
+    got_b = [start(sb.at[slot_of(lax.rem(y + d, NY))], rb2.at[d - 1], at_y(d)) for d in FAR_FIRST]
     for copy in got_a + got_b:
         copy.wait_recv()
     low_half = sa[z]
@@ -420,7 +424,7 @@
     sfull[y, 0:32, zcols] = low_half.astype(BF)
     sfull[y, 32:64, zcols] = high_half.astype(BF)
     got_a, got_b = [], []
-    for d in range(1, 8):
+    for d in FAR_FIRST:
         got_a.append(start(sfull.at[y, 0:32, zcols], sfull.at[y, 0:32, zcols], at_z(d)))
         got_b.append(start(sfull.at[y, 32:64, zcols], sfull.at[y, 32:64, zcols], at_y(d)))
 
@@ -428,14 +432,14 @@
     twice = jnp.concatenate([part, part], axis=0)
     gram = dot_nt(part, twice, HIGHEST)
     gs[...] = jnp.where(lanes((32, 128)) < 64, gram[0:32], gram[32:64])
-    got_gram = [start(gs, gr.at[d - 1], at_z(d)) for d in range(1, 8)]
+    got_gram = [start(gs, gr.at[d - 1], at_z(d)) for d in FAR_FIRST]
 
     for copy in got_a:
         copy.wait_recv()
-    spread = [start(sfull.at[y, 0:32], sfull.at[y, 0:32], at_y(d)) for d in range(1, 8)]
+    spread = [start(sfull.at[y, 0:32], sfull.at[y, 0:32], at_y(d)) for d in FAR_FIRST]
     for copy in got_b:
         copy.wait_recv()
-    spread += [start(sfull.at[:, 32:64, zcols], sfull.at[:, 32:64, zcols], at_z(d)) for d in range(1, 8)]
+    spread += [start(sfull.at[:, 32:64, zcols], sfull.at[:, 32:64, zcols], at_z(d)) for d in FAR_FIRST]
 
     blocks = []
 
@@ -456,13 +460,15 @@
     for copy in spread:
         copy.wait_recv()
 
-    for j in range(0, 8, 2):
-        value = dot_nt(sfull[j : j + 2].reshape(128, 1024), lum[...]).astype(BF)
-        ut[j] = value[0:64]
-        ut[j + 1] = value[64:128]
     came = {}
-    for q, par in others:
-        came[back[(q, par)]] = start(ut.at[res_of(q, par)], utr.at[back[(q, par)]], at_res(q, par))
+    for q in (2, 1, 3, 0):
+        chip = lax.rem(x + q, NX)
+        value = dot_nt(sfull[pl.ds(2 * chip, 2)].reshape(128, 1024), lum[...]).astype(BF)
+        ut[2 * chip] = value[0:64]
+        ut[2 * chip + 1] = value[64:128]
+        for par in range(2):
+            if (q, par) != (0, 0):
+                came[back[(q, par)]] = start(ut.at[res_of(q, par)], utr.at[back[(q, par)]], at_res(q, par))
     utr[0] = ut[r]
     row_cols = pl.ds(pl.multiple_of(y * 128, 128), 128)
     rows_came = []
@@ -471,7 +477,7 @@
     srr[0] = sfull[r, :, row_cols]
     eliminate(blocks, 40, 64)
     linvg[y] = inverse_of(blocks)
-    got_inverse = [start(linvg.at[y], linvg.at[y], at_y(d)) for d in range(1, 8)]
+    got_inverse = [start(linvg.at[y], linvg.at[y], at_y(d)) for d in FAR_FIRST]
 
     for slot in range(4):
         if slot:
@@ -481,7 +487,7 @@
             for t in range(2):
                 tile = part[:, 128 * t : 128 * t + 128]
                 ia[2 * n + t, 64 * slot : 64 * slot + 64, :] = tile.astype(BF)
-    got_a = [start(ia.at[lax.rem(y + d, NY)], ria.at[d - 1], at_y(d)) for d in range(1, 8)]
+    got_a = [start(ia.at[lax.rem(y + d, NY)], ria.at[d - 1], at_y(d)) for d in FAR_FIRST]
     for pair in (1, 0):
         slot = 4 + 2 * pair
         came[slot].wait_recv()
@@ -494,7 +500,7 @@
             for t in range(2):
                 turned = part[:, 128 * t : 128 * t + 128].T.astype(BF)
                 ib[:, 2 * n + t, :, 128 * pair : 128 * pair + 128] = turned.reshape(8, 16, 128)
-    got_b = [start(ib.at[lax.rem(z + d, NZ)], rib.at[d - 1], at_z(d)) for d in range(1, 8)]
+    got_b = [start(ib.at[lax.rem(z + d, NZ)], rib.at[d - 1], at_z(d)) for d in FAR_FIRST]
     for copy in got_inverse:
         copy.wait_recv()
     inverse_came = []
@@ -507,7 +513,7 @@
     for d in range(7):
         total = total + ria[d].astype(F32)
     fa[...] = total.T.reshape(8, 16, 256)
-    got_a = [start(fa.at[lax.rem(z + d, NZ)], ria2.at[d - 1], at_z(d)) for d in range(1, 8)]
+    got_a = [start(fa.at[lax.rem(z + d, NZ)], ria2.at[d - 1], at_z(d)) for d in FAR_FIRST]
     for copy in got_b:
         copy.wait_recv()
     for n in range(8):
@@ -515,7 +521,7 @@
         for d in range(7):
             total = total + rib[d, n].astype(F32)
         fb[n] = total
-    got_b = [start(fb.at[lax.rem(y + d, NY)], rib2.at[d - 1], at_y(d)) for d in range(1, 8)]
+    got_b = [start(fb.at[lax.rem(y + d, NY)], rib2.at[d - 1], at_y(d)) for d in FAR_FIRST]
 
     for copy in rows_came + inverse_came:
         copy.wait_recv()

time: 115 us -> 110 us (0.957)
  Pallas kernels: 111 us -> 106 us
    pallas_call x1, Pallas kernels: 111 us -> 106 us  [local(): pl.pallas_call(kernel, out_shape=[jax.ShapeDtypeStruct((8, 16, 64), F32)]...]
where the time goes in v4:
time: 110 us
  Pallas kernels  106 us (96%)
  local copies, waits for them, and re-layouts  2.95 us (3%)
  between operations  1.29 us (1%)
    pallas_call x1, Pallas kernels, local(): pl.pallas_call(kernel, out_shape=[jax.ShapeDtypeStruct((8, 16, 64), F32)]...  106 us
    unnamed x2, local copies, waits for them, and re-layouts  2.95 us

profile of v4, /device:TPU:1, one launch (start us, length us, event | category | flops | bytes accessed | tf_op | source)
XLA Modules:
  0.0 110.1 jit_solution(8590287780657008139)
XLA Ops:
  1.3 105.8 %shard_map.113 = (f32[8,16,64]{2,1,0:T(8,128)}, f32[8,16,64]{2,1,0:T(8,128)}) custom-call(bf16[4,64,1024]{2,1,0:T(8,128)(2,1)} %bitcast.25, bf16[4,64,1024]{2,1,0:T(8,128)(2,1)} %bitcast.26, bf16[4,64,1024]{2,1,0:T(8,128)(2,1)} %bitcast.27, bf16[4,64,1024]{2,1,0:T(8,128)(2,1)} %bitcast.28, bf16[1024,1024]{1,0:T(8,128)(2,1)} %bitcast.24, ...), custom_call_target="tpu_custom_call" | custom-call | tf_op jit(solution)/shard_map/pallas_call | solution.py:611
  107.1 1.5 %copy.17 = f32[8,1,16,64]{3,2,1,0:T(8,128)} copy(f32[8,1,16,64]{3,2,1,0:T(8,128)} %bitcast.31) | data formatting | bytes 65536
  108.6 1.5 %copy.18 = f32[8,1,16,64]{3,2,1,0:T(8,128)} copy(f32[8,1,16,64]{3,2,1,0:T(8,128)} %bitcast.30) | data formatting | bytes 65536

commit v5 on v4

--- a/solution.py
+++ b/solution.py
@@ -383,12 +383,13 @@
     expand_and_send(3)
     expand_and_send(1)
     sketch_chip(0)
+    send_high(slice(0, 2))
     for k in (0, 2, 1, 3):
         forward(2, k)
     expand_and_send(2)
     sketch_chip(3)
     sketch_chip(1)
-    send_high(slice(0, 6))
+    send_high(slice(2, 6))
     sketch_chip(2)
     send_high(slice(6, 8))
     for piece in weight_work:

time: 110 us -> 111 us (level)
  no operation moved by 1% of the time
where the time goes in v5:
time: 111 us
  Pallas kernels  106 us (95%)
  local copies, waits for them, and re-layouts  2.95 us (3%)
  between operations  1.29 us (1%)
    pallas_call x1, Pallas kernels, local(): pl.pallas_call(kernel, out_shape=[jax.ShapeDtypeStruct((8, 16, 64), F32)]...  106 us
    unnamed x2, local copies, waits for them, and re-layouts  2.95 us

profile of v5, /device:TPU:1, one launch (start us, length us, event | category | flops | bytes accessed | tf_op | source)
XLA Modules:
  0.0 110.7 jit_solution(5435666453147277259)
XLA Ops:
  1.3 106.4 %shard_map.113 = (f32[8,16,64]{2,1,0:T(8,128)}, f32[8,16,64]{2,1,0:T(8,128)}) custom-call(bf16[4,64,1024]{2,1,0:T(8,128)(2,1)} %bitcast.25, bf16[4,64,1024]{2,1,0:T(8,128)(2,1)} %bitcast.26, bf16[4,64,1024]{2,1,0:T(8,128)(2,1)} %bitcast.27, bf16[4,64,1024]{2,1,0:T(8,128)(2,1)} %bitcast.28, bf16[1024,1024]{1,0:T(8,128)(2,1)} %bitcast.24, ...), custom_call_target="tpu_custom_call" | custom-call | tf_op jit(solution)/shard_map/pallas_call | solution.py:612
  107.7 1.5 %copy.17 = f32[8,1,16,64]{3,2,1,0:T(8,128)} copy(f32[8,1,16,64]{3,2,1,0:T(8,128)} %bitcast.31) | data formatting | bytes 65536
  109.2 1.5 %copy.18 = f32[8,1,16,64]{3,2,1,0:T(8,128)} copy(f32[8,1,16,64]{3,2,1,0:T(8,128)} %bitcast.30) | data formatting | bytes 65536
